TPU v7x, 32 devices: a whole 2x2x4 slice. The times are simulated.
32 devices in a mesh: row: 8 (over y, x, core), col: 4 (over z).
Axes of the slice: x: 2, y: 2, z: 4, core: 2. Of those that a mesh axis runs over, the one named last changes fastest.
Arguments:
- specimen_transmit: float32 [2, 2, 2048, 1024], P(None, None, 'row', 'col'), may hold values from -5 to 5
- illumination: float32 [2, 256, 256], replicated, may hold values from -5 to 5
- fresnel_angle: float32 [256, 256], replicated, may hold values from -3.140625 to 3.140625
- recorded_intensity: float32 [8, 4, 2, 256, 256], P('row', 'col'), may hold values from 0.1 to 3
- frame_shifts: int32 [8, 4, 2, 2], P('row', 'col'), may hold values from -128 to 128, as said below
Outputs:
- obj_grad: float32 [2, 2, 2048, 1024], P(None, None, 'row', 'col')
- probe_grad: float32 [2, 256, 256], P(None, 'row', 'col')
Inputs may be any that keep to these rules, and one draw needn't show every extreme that they name: `frame_shifts`: shifts stay within the margin, so a window reaches only its own tile and the eight tiles around it; both ends of the range occur in every draw.
All inputs are finite; a program needn't handle non-finite values.
Results may differ from a plain program's by a relative error of at most 0.0003.
Values sent between devices are 32-bit elements; how exact they have to be, the bound alone decides.
A program may use at most 128 MiB of HBM per device.

v0:
```python
import functools
import math

import jax
import jax.numpy as jnp
import ml_dtypes
import numpy as np
from jax import lax
from jax.experimental import pallas as pl
from jax.experimental.pallas import tpu as pltpu
from jax.sharding import PartitionSpec as P

HALO = 128
ROWS = 8
F32 = jnp.float32
BF16 = jnp.bfloat16


def make_tables(width):
    index = np.arange(width)
    angle = (index[:, None] * index[None, :] % width) * (2.0 * math.pi / width)
    both = np.concatenate([np.cos(angle), np.sin(angle)], axis=0) / math.sqrt(width)
    high = both.astype(ml_dtypes.bfloat16)
    low = (both - high.astype(np.float64)).astype(ml_dtypes.bfloat16)
    right = np.concatenate([high, high, low], axis=0)
    return jnp.asarray(right), jnp.asarray(np.ascontiguousarray(right.T))


def split_field(field):
    high = field.astype(BF16)
    low = (field - high.astype(F32)).astype(BF16)
    return high, low


def transform(real_part, imag_part, right, left, forward):
    width = real_part.shape[0]

    def arrange(r, i, axis):
        if forward:
            top = jnp.concatenate([r, i], axis=axis)
            bottom = jnp.concatenate([i, -r], axis=axis)
        else:
            top = jnp.concatenate([r, -i], axis=axis)
            bottom = jnp.concatenate([i, r], axis=axis)
        return jnp.concatenate([top, bottom], axis=1 - axis)

    rh, rl = split_field(real_part)
    ih, il = split_field(imag_part)
    high = arrange(rh, ih, 1)
    field = jnp.concatenate([high, arrange(rl, il, 1), high], axis=1)
    mid = jnp.dot(field, right[...], preferred_element_type=F32)
    rh, rl = split_field(mid[:width])
    ih, il = split_field(mid[width:])
    high = arrange(rh, ih, 0)
    field = jnp.concatenate([high, arrange(rl, il, 0), high], axis=0)
    out = jnp.dot(left[...], field, preferred_element_type=F32)
    return out[:, :width], out[:, width:]


def complex_product(a_real, a_imag, b_real, b_imag):
    return (a_real * b_real - a_imag * b_imag, a_real * b_imag + a_imag * b_real)


def conj_product(a_real, a_imag, b_real, b_imag):
    return (a_real * b_real + a_imag * b_imag, a_real * b_imag - a_imag * b_real)


def local_kernel(
    layers, shifts, mid, west, east, north, south, ncorn, scorn, illum, filt, seen, right, left,
    g_mid, g_west, g_east, g_north, g_south, g_ncorn, g_scorn, g_probe,
    ext, acc, win,
):
    tile = mid.shape[1]
    width = illum.shape[1]
    places = seen.shape[0]
    a, b = HALO, HALO + tile
    e = b + HALO
    parts = (
        (mid, slice(a, b), slice(a, b), None),
        (west, slice(a, b), slice(0, a), None),
        (east, slice(a, b), slice(b, e), None),
        (north, slice(0, a), slice(a, b), None),
        (south, slice(b, e), slice(a, b), None),
        (ncorn, slice(0, a), slice(0, a), 0),
        (ncorn, slice(0, a), slice(b, e), 1),
        (scorn, slice(b, e), slice(0, a), 0),
        (scorn, slice(b, e), slice(b, e), 1),
    )
    for ref, rows, cols, side in parts:
        ext[:, rows, cols] = ref[...] if side is None else ref[side]
    acc[...] = jnp.zeros_like(acc)
    g_probe[...] = jnp.zeros_like(g_probe)

    @pl.loop(0, places)
    def _(p):
        start_row = shifts[p, 0] + HALO
        start_col = shifts[p, 1] + HALO
        block = jnp.where(start_col > HALO, 1, 0)
        base = pl.multiple_of(block * HALO, HALO)
        rest = start_col - base
        span = width + HALO
        first = pl.multiple_of(start_row // ROWS * ROWS, ROWS)
        over = start_row - first
        tall = width + ROWS
        rows = pl.ds(first, tall)
        for c in range(2 * layers):
            wide = ext[c, rows, pl.ds(base, span)]
            wide = pltpu.roll(wide, lax.rem(tall - over, tall), 0)[:width]
            win[c] = pltpu.roll(wide, lax.rem(span - rest, span), 1)[:, :width]
        wave = (illum[0], illum[1])
        saved = []
        for layer in range(layers):
            saved.append(wave)
            out = complex_product(*wave, win[2 * layer], win[2 * layer + 1])
            if layer + 1 < layers:
                spec = transform(*out, right, left, True)
                spec = complex_product(*spec, filt[0], filt[1])
                wave = transform(*spec, right, left, False)
        far_real, far_imag = transform(*out, right, left, True)
        misfit = far_real * far_real + far_imag * far_imag - seen[p]
        back = transform(misfit * far_real, misfit * far_imag, right, left, False)
        for layer in reversed(range(layers)):
            grads = conj_product(*saved[layer], *back)
            for k in range(2):
                wide = jnp.concatenate([grads[k], jnp.zeros((width, HALO), F32)], axis=1)
                wide = pltpu.roll(wide, rest, 1)
                wide = jnp.concatenate([wide, jnp.zeros((ROWS, span), F32)], axis=0)
                wide = pltpu.roll(wide, over, 0)
                acc[2 * layer + k, rows, pl.ds(base, span)] += wide
            head = conj_product(win[2 * layer], win[2 * layer + 1], *back)
            if layer > 0:
                spec = transform(*head, right, left, True)
                spec = conj_product(filt[0], filt[1], *spec)
                back = transform(*spec, right, left, False)
        g_probe[0] += head[0]
        g_probe[1] += head[1]

    outs = (g_mid, g_west, g_east, g_north, g_south, g_ncorn, g_ncorn, g_scorn, g_scorn)
    for (_, rows, cols, side), out in zip(parts, outs):
        if side is None:
            out[...] = acc[:, rows, cols]
        else:
            out[side] = acc[:, rows, cols]


def local_gradients(layers, shifts, pieces, illum, filt, seen, right, left):
    chans, tile = pieces[0].shape[:2]
    width = illum.shape[1]
    side = tile + 2 * HALO
    vmem = pl.BlockSpec(memory_space=pltpu.VMEM)
    shapes = [x.shape for x in pieces] + [illum.shape]
    return pl.pallas_call(
        functools.partial(local_kernel, layers),
        out_shape=[jax.ShapeDtypeStruct(s, F32) for s in shapes],
        in_specs=[pl.BlockSpec(memory_space=pltpu.SMEM)] + [vmem] * 12,
        out_specs=[vmem] * 8,
        scratch_shapes=[
            pltpu.VMEM((chans, side + ROWS, side), F32),
            pltpu.VMEM((chans, side + ROWS, side), F32),
            pltpu.VMEM((chans, width, width), F32),
        ],
        compiler_params=pltpu.CompilerParams(vmem_limit_bytes=56 * 2**20),
        name="local_gradients",
    )(shifts, *pieces, illum, filt, seen, right, left)


def ring(axis):
    count = lax.axis_size(axis)
    up = [(i, (i + 1) % count) for i in range(count)]
    return up, [(t, s) for s, t in up]


def body(specimen_transmit, illumination, fresnel_angle, recorded_intensity, frame_shifts):
    layers = specimen_transmit.shape[0]
    tile = specimen_transmit.shape[2]
    width = illumination.shape[1]
    right, left = make_tables(width)
    filt = jnp.stack([jnp.cos(fresnel_angle), jnp.sin(fresnel_angle)])
    mid = specimen_transmit.reshape(2 * layers, tile, specimen_transmit.shape[3])
    row_up, row_down = ring("row")
    col_up, col_down = ring("col")
    west = lax.ppermute(mid[:, :, -HALO:], "col", col_up)
    east = lax.ppermute(mid[:, :, :HALO], "col", col_down)
    north = lax.ppermute(mid[:, -HALO:], "row", row_up)
    south = lax.ppermute(mid[:, :HALO], "row", row_down)
    sides = jnp.stack([west, east])
    ncorn = lax.ppermute(sides[:, :, -HALO:], "row", row_up)
    scorn = lax.ppermute(sides[:, :, :HALO], "row", row_down)
    pieces = (mid, west, east, north, south, ncorn, scorn)
    g_mid, g_west, g_east, g_north, g_south, g_ncorn, g_scorn, g_probe = local_gradients(
        layers, frame_shifts[0, 0], pieces, illumination, filt, recorded_intensity[0, 0], right, left
    )
    from_south = lax.ppermute(g_ncorn, "row", row_down)
    from_north = lax.ppermute(g_scorn, "row", row_up)
    mid_south = lax.ppermute(g_north, "row", row_down)
    mid_north = lax.ppermute(g_south, "row", row_up)
    sides = jnp.stack([g_west, g_east])
    sides = sides.at[:, :, -HALO:].add(from_south)
    sides = sides.at[:, :, :HALO].add(from_north)
    from_east = lax.ppermute(sides[0], "col", col_down)
    from_west = lax.ppermute(sides[1], "col", col_up)
    far = tile - HALO

    def fit(x, low_row, low_col):
        rows, cols = x.shape[1:]
        pads = ((0, 0), (low_row, tile - rows - low_row), (low_col, tile - cols - low_col))
        return jnp.pad(x, pads)

    result = (
        g_mid
        + fit(mid_south, far, 0)
        + fit(mid_north, 0, 0)
        + fit(from_east, 0, far)
        + fit(from_west, 0, 0)
    )
    result = result.reshape(specimen_transmit.shape)
    partial_rows = lax.psum_scatter(g_probe, "row", scatter_dimension=1, tiled=True)
    probe_part = lax.psum_scatter(partial_rows, "col", scatter_dimension=2, tiled=True)
    return (result, probe_part)


def solution(mesh):
    placed = (
        P(None, None, "row", "col"),
        P(),
        P(),
        P("row", "col", None, None, None),
        P("row", "col", None, None),
    )
    return jax.shard_map(
        body,
        mesh=mesh,
        in_specs=placed,
        out_specs=(P(None, None, "row", "col"), P(None, "row", "col")),
        check_vma=False,
    )
```

profile of v0, /device:TPU:0, one launch (start us, length us, event | category | flops | bytes accessed | tf_op | source)
XLA Modules:
  0.0 151.3 jit_solution(7197292608356146302)
XLA Ops:
  7.2 0.0 reduce-scatter.5.cloned.1.call-start
  7.2 0.0 copy-start
  7.2 1.4 fusion.6
  8.6 5.1 %collective-permute-start.1 = (f32[4,256,128]{2,1,0:T(8,128)S(1)}, f32[4,256,128]{2,1,0:T(8,128)S(1)}, u32[]{:S(2)}, u32[]{:S(2)}) collective-permute-start(f32[4,256,128]{2,1,0:T(8,128)S(1)} %get-tuple-element.48), channel_id=1, source_target_pairs={{1,0},{2,1},{3,2},{0,3},{5,4},{6,5},{7,6},{4,7},{9,8},{10,9},{11,1... | collective-permute-start | bytes 1572872 | tf_op jit(solution)/shard_map/ppermute | solution.py:183
  13.7 0.0 collective-permute-start
  13.7 0.0 copy-done
  13.7 0.1 fusion.5
  13.8 1.7 %collective-permute-start.3 = (f32[4,128,256]{2,1,0:T(8,128)S(1)}, f32[4,128,256]{2,1,0:T(8,128)S(1)}, u32[]{:S(2)}, u32[]{:S(2)}) collective-permute-start(f32[4,128,256]{2,1,0:T(8,128)S(1)} %get-tuple-element.46), channel_id=1, source_target_pairs={{4,0},{8,4},{12,8},{16,12},{20,16},{24,20},{28,24},{0,28},{5,1},{9... | collective-permute-start | bytes 1572872 | tf_op jit(solution)/shard_map/ppermute | solution.py:185
  15.4 0.0 collective-permute-start.2
  15.4 10.6 %collective-permute-done.1.east = f32[4,256,128]{2,1,0:T(8,128)S(1)} collective-permute-done((f32[4,256,128]{2,1,0:T(8,128)S(1)}, f32[4,256,128]{2,1,0:T(8,128)S(1)}, u32[]{:S(2)}, u32[]{:S(2)}) %collective-permute-start.1) | collective-permute-done | bytes 524320 | tf_op jit(solution)/shard_map/ppermute | solution.py:183
  26.0 11.0 %collective-permute-done.west = f32[4,256,128]{2,1,0:T(8,128)S(1)} collective-permute-done((f32[4,256,128]{2,1,0:T(8,128)S(1)}, f32[4,256,128]{2,1,0:T(8,128)S(1)}, u32[]{:S(2)}, u32[]{:S(2)}) %collective-permute-start) | collective-permute-done | bytes 524320 | tf_op jit(solution)/shard_map/ppermute | solution.py:182
  37.0 0.0 copy-start.4
  37.0 0.0 copy-start.10
  37.0 0.1 pad_maximum_fusion.1
  37.1 0.0 copy-done.3
  37.1 0.7 copy-done.4
  37.8 1.0 collective-permute-start.5
  38.8 0.0 collective-permute-start.4
  38.8 0.0 copy-done.10
  38.8 0.9 cosine_bitcast_fusion
  39.8 0.8 pad_maximum_fusion.2.filt
  40.6 0.0 collective-permute-done.3.south
  40.6 0.0 copy-start.6
  40.6 0.0 collective-permute-done.2.north
  40.6 0.0 copy-start.7
  40.6 10.4 %collective-permute-done.5.scorn = f32[2,4,128,128]{3,2,1,0:T(8,128)S(1)} collective-permute-done((f32[2,4,128,128]{3,2,1,0:T(8,128)S(1)}, f32[2,4,128,128]{3,2,1,0:T(8,128)S(1)}, u32[]{:S(2)}, u32[]{:S(2)}) %collective-permute-start.5) | collective-permute-done | bytes 524320 | tf_op jit(solution)/shard_map/ppermute | solution.py:188
  51.0 0.0 copy-start.8
  51.0 2.0 %collective-permute-done.4.ncorn = f32[2,4,128,128]{3,2,1,0:T(8,128)S(1)} collective-permute-done((f32[2,4,128,128]{3,2,1,0:T(8,128)S(1)}, f32[2,4,128,128]{3,2,1,0:T(8,128)S(1)}, u32[]{:S(2)}, u32[]{:S(2)}) %collective-permute-start.4) | collective-permute-done | bytes 524320 | tf_op jit(solution)/shard_map/ppermute | solution.py:187
  53.0 0.0 copy-start.9
  53.0 0.0 copy-done.6
  53.0 0.0 copy-done.7
  53.0 0.0 copy-done.8
  53.0 0.8 copy-done.9
  53.8 29.7 %local_gradients.1 = (f32[4,256,256]{2,1,0:T(8,128)}, f32[4,256,128]{2,1,0:T(8,128)}, f32[4,256,128]{2,1,0:T(8,128)}, f32[4,128,256]{2,1,0:T(8,128)}, f32[4,128,...) custom-call(s32[2,2]{1,0:T(2,128)} %bitcast.31, ...), custom_call_target="tpu_custom_call" | custom-call | tf_op jit(solution)/shard_map/local_gradients/pallas_call | solution.py:152
  83.6 1.1 collective-permute-start.8
  84.6 0.0 collective-permute-start.9
  84.6 0.0 reduce-scatter.5.cloned.1.call-update
  84.7 0.0 reduce-scatter.7.cloned.1.call-start
  84.7 2.7 %collective-permute-start.6 = (f32[4,128,256]{2,1,0:T(8,128)}, f32[4,128,256]{2,1,0:T(8,128)S(1)}, u32[]{:S(2)}, u32[]{:S(2)}) collective-permute-start(f32[4,128,256]{2,1,0:T(8,128)} %get-tuple-element.35), channel_id=1, source_target_pairs={{4,0},{8,4},{12,8},{16,12},{20,16},{24,20},{28,24},{0,28},{5,1},{9... | collective-permute-start | bytes 1572872 | tf_op jit(solution)/shard_map/ppermute | solution.py:195
  87.4 0.0 collective-permute-start.7
  87.4 0.0 copy-done.1
  87.4 1.2 pad_maximum_fusion
  88.6 8.7 %collective-permute-done.8 = f32[2,4,128,128]{3,2,1,0:T(8,128)S(1)} collective-permute-done((f32[2,4,128,128]{3,2,1,0:T(8,128)}, f32[2,4,128,128]{3,2,1,0:T(8,128)S(1)}, u32[]{:S(2)}, u32[]{:S(2)}) %collective-permute-start.8) | collective-permute-done | bytes 524320 | tf_op jit(solution)/shard_map/ppermute | solution.py:193
  97.3 0.0 copy-done.2
  97.3 0.1 fusion.3
  97.3 2.7 %collective-permute-done.9 = f32[2,4,128,128]{3,2,1,0:T(8,128)S(1)} collective-permute-done((f32[2,4,128,128]{3,2,1,0:T(8,128)}, f32[2,4,128,128]{3,2,1,0:T(8,128)S(1)}, u32[]{:S(2)}, u32[]{:S(2)}) %collective-permute-start.9) | collective-permute-done | bytes 524320 | tf_op jit(solution)/shard_map/ppermute | solution.py:194
  100.0 0.1 fusion.4
  100.2 0.1 slice_bitcast_fusion.1
  100.2 0.0 copy-start.5
  100.2 1.4 collective-permute-start.10
  101.6 0.7 collective-permute-start.11
  102.3 16.7 %reduce-scatter.5.cloned.1.call-done = f32[2,32,256]{2,1,0:T(8,128)} async-done(((f32[2,256,256]{2,1,0:T(8,128)}), f32[2,32,256]{2,1,0:T(8,128)}) %reduce-scatter.5.cloned.1.call-update) | async-done | bytes 65552 | tf_op jit(solution)/shard_map/reduce_scatter | solution.py:217
  119.0 1.0 copy.9
  120.0 0.8 reshape.82
  120.8 0.0 reduce-scatter.7.cloned.1.call-update
  120.8 19.7 %reduce-scatter.7.cloned.1.call-done = f32[64,64]{1,0:T(8,128)} async-done(((f32[256,64]{1,0:T(8,128)}), f32[64,64]{1,0:T(8,128)}) %reduce-scatter.7.cloned.1.call-update) | async-done | bytes 16400
  140.5 0.9 reshape.83
  141.4 0.7 copy.10
  142.1 0.0 collective-permute-done.6
  142.1 0.0 collective-permute-done.7
  142.1 0.0 collective-permute-done.10
  142.1 0.0 collective-permute-done.11
  142.1 0.0 copy-done.5
  142.1 2.3 %pad_add_fusion = f32[4,256,256]{2,1,0:T(8,128)} fusion(f32[4,256,128]{2,1,0:T(8,128)} %collective-permute-done.11, f32[4,256,128]{2,1,0:T(8,128)} %collective-permute-done.10, f32[4,128,256]{2,1,0:T(8,128)S(1)} %collective-permute-done.7, f32[4,256,256]{2,1,0:T(8,128)S(1)} %copy-done.5, f32[4,128,256]{2,1,0:T(8,128)S(1)} %collective-permute-done.6), kind=kLoop, calls=%fused_computation.5 | loop fusion | flops 1048576 | bytes 4194304 | tf_op jit(solution)/shard_map/add | solution.py:210
  (3 shorter events, 0.0 us)
Async XLA Ops:
  7.2 111.8 %reduce-scatter.5.cloned.1.call-start = ((), (), s32[]{:S(2)}) async-start(), calls=%async_computation.2 | async-start | bytes 589824 | tf_op jit(solution)/shard_map/reduce_scatter | solution.py:217
  7.2 6.5 %copy-start = (f32[2,2,256,256]{3,2,1,0:T(8,128)S(1)}, f32[2,2,256,256]{3,2,1,0:T(8,128)}, u32[]{:S(2)}) copy-start(f32[2,2,256,256]{3,2,1,0:T(8,128)} %param.11) | copy-start | bytes 3145732
  8.6 17.4 %collective-permute-start.1 = (f32[4,256,128]{2,1,0:T(8,128)S(1)}, f32[4,256,128]{2,1,0:T(8,128)S(1)}, u32[]{:S(2)}, u32[]{:S(2)}) collective-permute-start(f32[4,256,128]{2,1,0:T(8,128)S(1)} %get-tuple-element.48), channel_id=1, source_target_pairs={{1,0},{2,1},{3,2},{0,3},{5,4},{6,5},{7,6},{4,7},{9,8},{10,9},{11,1... | collective-permute-start | bytes 1572872 | tf_op jit(solution)/shard_map/ppermute | solution.py:183
  13.7 23.3 %collective-permute-start = (f32[4,256,128]{2,1,0:T(8,128)S(1)}, f32[4,256,128]{2,1,0:T(8,128)S(1)}, u32[]{:S(2)}, u32[]{:S(2)}) collective-permute-start(f32[4,256,128]{2,1,0:T(8,128)S(1)} %get-tuple-element.49), channel_id=1, source_target_pairs={{0,1},{1,2},{2,3},{3,0},{4,5},{5,6},{6,7},{7,4},{8,9},{9,10},{10,1... | collective-permute-start | bytes 1572872 | tf_op jit(solution)/shard_map/ppermute | solution.py:182
  13.8 26.8 %collective-permute-start.3 = (f32[4,128,256]{2,1,0:T(8,128)S(1)}, f32[4,128,256]{2,1,0:T(8,128)S(1)}, u32[]{:S(2)}, u32[]{:S(2)}) collective-permute-start(f32[4,128,256]{2,1,0:T(8,128)S(1)} %get-tuple-element.46), channel_id=1, source_target_pairs={{4,0},{8,4},{12,8},{16,12},{20,16},{24,20},{28,24},{0,28},{5,1},{9... | collective-permute-start | bytes 1572872 | tf_op jit(solution)/shard_map/ppermute | solution.py:185
  15.4 25.2 %collective-permute-start.2 = (f32[4,128,256]{2,1,0:T(8,128)S(1)}, f32[4,128,256]{2,1,0:T(8,128)S(1)}, u32[]{:S(2)}, u32[]{:S(2)}) collective-permute-start(f32[4,128,256]{2,1,0:T(8,128)S(1)} %get-tuple-element.47), channel_id=1, source_target_pairs={{0,4},{4,8},{8,12},{12,16},{16,20},{20,24},{24,28},{28,0},{1,5},{5... | collective-permute-start | bytes 1572872 | tf_op jit(solution)/shard_map/ppermute | solution.py:184
  26.0 11.1 %copy-start.3 = (f32[4,256,128]{2,1,0:T(8,128)}, f32[4,256,128]{2,1,0:T(8,128)S(1)}, u32[]{:S(2)}) copy-start(f32[4,256,128]{2,1,0:T(8,128)S(1)} %collective-permute-done.1.east) | copy-start | bytes 1572868
  37.0 0.8 copy-start.4
  37.0 1.8 %copy-start.10 = (f32[256,256]{1,0:T(8,128)S(1)}, f32[256,256]{1,0:T(8,128)}, u32[]{:S(2)}) copy-start(f32[256,256]{1,0:T(8,128)} %param.13) | copy-start | bytes 786436
  37.8 13.2 %collective-permute-start.5 = (f32[2,4,128,128]{3,2,1,0:T(8,128)S(1)}, f32[2,4,128,128]{3,2,1,0:T(8,128)S(1)}, u32[]{:S(2)}, u32[]{:S(2)}) collective-permute-start(f32[2,4,128,128]{3,2,1,0:T(8,128)S(1)} %get-tuple-element.44), channel_id=1, source_target_pairs={{4,0},{8,4},{12,8},{16,12},{20,16},{24,20},{28,24},{0,28},{5,1},{9... | collective-permute-start | bytes 1572872 | tf_op jit(solution)/shard_map/ppermute | solution.py:188
  38.8 14.2 %collective-permute-start.4 = (f32[2,4,128,128]{3,2,1,0:T(8,128)S(1)}, f32[2,4,128,128]{3,2,1,0:T(8,128)S(1)}, u32[]{:S(2)}, u32[]{:S(2)}) collective-permute-start(f32[2,4,128,128]{3,2,1,0:T(8,128)S(1)} %get-tuple-element.45), channel_id=1, source_target_pairs={{0,4},{4,8},{8,12},{12,16},{16,20},{20,24},{24,28},{28,0},{1,5},{5... | collective-permute-start | bytes 1572872 | tf_op jit(solution)/shard_map/ppermute | solution.py:187
  40.6 12.4 %copy-start.6 = (f32[4,128,256]{2,1,0:T(8,128)}, f32[4,128,256]{2,1,0:T(8,128)S(1)}, u32[]{:S(2)}) copy-start(f32[4,128,256]{2,1,0:T(8,128)S(1)} %collective-permute-done.3.south) | copy-start | bytes 1572868
  40.6 12.4 %copy-start.7 = (f32[4,128,256]{2,1,0:T(8,128)}, f32[4,128,256]{2,1,0:T(8,128)S(1)}, u32[]{:S(2)}) copy-start(f32[4,128,256]{2,1,0:T(8,128)S(1)} %collective-permute-done.2.north) | copy-start | bytes 1572868
  51.0 2.0 %copy-start.8 = (f32[2,4,128,128]{3,2,1,0:T(8,128)}, f32[2,4,128,128]{3,2,1,0:T(8,128)S(1)}, u32[]{:S(2)}) copy-start(f32[2,4,128,128]{3,2,1,0:T(8,128)S(1)} %collective-permute-done.5.scorn) | copy-start | bytes 1572868
  53.0 0.8 copy-start.9
  83.6 3.8 %copy-start.1 = (f32[4,256,128]{2,1,0:T(8,128)S(1)}, f32[4,256,128]{2,1,0:T(8,128)}, u32[]{:S(2)}) copy-start(f32[4,256,128]{2,1,0:T(8,128)} %get-tuple-element.37) | copy-start | bytes 1572868
  83.6 13.7 %collective-permute-start.8 = (f32[2,4,128,128]{3,2,1,0:T(8,128)}, f32[2,4,128,128]{3,2,1,0:T(8,128)S(1)}, u32[]{:S(2)}, u32[]{:S(2)}) collective-permute-start(f32[2,4,128,128]{3,2,1,0:T(8,128)} %get-tuple-element.39), channel_id=1, source_target_pairs={{4,0},{8,4},{12,8},{16,12},{20,16},{24,20},{28,24},{0,28},{5,1},{9... | collective-permute-start | bytes 1572872 | tf_op jit(solution)/shard_map/ppermute | solution.py:193
  84.6 15.4 %collective-permute-start.9 = (f32[2,4,128,128]{3,2,1,0:T(8,128)}, f32[2,4,128,128]{3,2,1,0:T(8,128)S(1)}, u32[]{:S(2)}, u32[]{:S(2)}) collective-permute-start(f32[2,4,128,128]{3,2,1,0:T(8,128)} %get-tuple-element.40), channel_id=1, source_target_pairs={{0,4},{4,8},{8,12},{12,16},{16,20},{20,24},{24,28},{28,0},{1,5},{5... | collective-permute-start | bytes 1572872 | tf_op jit(solution)/shard_map/ppermute | solution.py:194
  84.7 55.9 %reduce-scatter.7.cloned.1.call-start = ((), (), s32[]{:S(2)}) async-start(), calls=%async_computation.3 | async-start | bytes 163840
  84.7 57.4 %collective-permute-start.6 = (f32[4,128,256]{2,1,0:T(8,128)}, f32[4,128,256]{2,1,0:T(8,128)S(1)}, u32[]{:S(2)}, u32[]{:S(2)}) collective-permute-start(f32[4,128,256]{2,1,0:T(8,128)} %get-tuple-element.35), channel_id=1, source_target_pairs={{4,0},{8,4},{12,8},{16,12},{20,16},{24,20},{28,24},{0,28},{5,1},{9... | collective-permute-start | bytes 1572872 | tf_op jit(solution)/shard_map/ppermute | solution.py:195
  87.4 54.7 %collective-permute-start.7 = (f32[4,128,256]{2,1,0:T(8,128)}, f32[4,128,256]{2,1,0:T(8,128)S(1)}, u32[]{:S(2)}, u32[]{:S(2)}) collective-permute-start(f32[4,128,256]{2,1,0:T(8,128)} %get-tuple-element.36), channel_id=1, source_target_pairs={{0,4},{4,8},{8,12},{12,16},{16,20},{20,24},{24,28},{28,0},{1,5},{5... | collective-permute-start | bytes 1572872 | tf_op jit(solution)/shard_map/ppermute | solution.py:196
  87.4 9.9 %copy-start.2 = (f32[4,256,128]{2,1,0:T(8,128)S(1)}, f32[4,256,128]{2,1,0:T(8,128)}, u32[]{:S(2)}) copy-start(f32[4,256,128]{2,1,0:T(8,128)} %get-tuple-element.38) | copy-start | bytes 1572868
  100.2 41.9 %copy-start.5 = (f32[4,256,256]{2,1,0:T(8,128)S(1)}, f32[4,256,256]{2,1,0:T(8,128)}, u32[]{:S(2)}) copy-start(f32[4,256,256]{2,1,0:T(8,128)} %get-tuple-element.34) | copy-start | bytes 3145732
  100.2 41.9 %collective-permute-start.10 = (f32[4,256,128]{2,1,0:T(8,128)S(1)}, f32[4,256,128]{2,1,0:T(8,128)}, u32[]{:S(2)}, u32[]{:S(2)}) collective-permute-start(f32[4,256,128]{2,1,0:T(8,128)S(1)} %get-tuple-element.42), channel_id=1, source_target_pairs={{1,0},{2,1},{3,2},{0,3},{5,4},{6,5},{7,6},{4,7},{9,8},{10,9},{11,1... | collective-permute-start | bytes 1572872 | tf_op jit(solution)/shard_map/ppermute | solution.py:200
  101.6 40.5 %collective-permute-start.11 = (f32[4,256,128]{2,1,0:T(8,128)S(1)}, f32[4,256,128]{2,1,0:T(8,128)}, u32[]{:S(2)}, u32[]{:S(2)}) collective-permute-start(f32[4,256,128]{2,1,0:T(8,128)S(1)} %get-tuple-element.43), channel_id=1, source_target_pairs={{0,1},{1,2},{2,3},{3,0},{4,5},{5,6},{6,7},{7,4},{8,9},{9,10},{10,1... | collective-permute-start | bytes 1572872 | tf_op jit(solution)/shard_map/ppermute | solution.py:201
Sparse Core Ops, SparseCore 0:
  84.8 34.1 reduce-scatter.4
  121.3 19.1 reduce-scatter.6
where the time goes:
time: 152 us; the launch traced here: 151 us
  waiting for transfers between devices  81.8 us (54%)
  Pallas kernels  29.7 us (20%)
  between operations  14.2 us (9%)
  starting transfers between devices  13.7 us (9%)
  local copies, waits for them, and re-layouts  7.31 us (5%)
  other arithmetic  4.63 us (3%)
    pallas_call x1, Pallas kernels, local_gradients(): pl.pallas_call(functools.partial(local_kernel, layers), out_shape=[jax.Sh...  29.7 us
    unnamed x3, waiting for transfers between devices  19.8 us
    reduce_scatter x1, waiting for transfers between devices, body(): lax.psum_scatter(g_probe, 'row', scatter_dimension=1, tiled=True)  16.7 us
    ppermute x1, waiting for transfers between devices, body(): west = lax.ppermute(mid[:, :, -HALO:], 'col', col_up)  11 us
    ppermute x1, waiting for transfers between devices, body(): east = lax.ppermute(mid[:, :, :HALO], 'col', col_down)  10.6 us
    ppermute x1, waiting for transfers between devices, body(): scorn = lax.ppermute(sides[:, :, :HALO], 'row', row_down)  10.4 us
    ppermute x1, waiting for transfers between devices, body(): from_south = lax.ppermute(g_ncorn, 'row', row_down)  8.68 us
    ppermute x1, starting transfers between devices, body(): east = lax.ppermute(mid[:, :, :HALO], 'col', col_down)  5.1 us
  transfers between devices with their start and end apart: 14, of which 8 were waited for; matrix products, arithmetic and copies ran while one was open for 4% of the time, Pallas kernels for 0%

commit v1 on v0

--- a/solution.py
+++ b/solution.py
@@ -164,10 +164,222 @@
     )(shifts, *pieces, illum, filt, seen, right, left)
 
 
-def ring(axis):
-    count = lax.axis_size(axis)
-    up = [(i, (i + 1) % count) for i in range(count)]
-    return up, [(t, s) for s, t in up]
+def remote(src, dst, sems, slot, device):
+    return pltpu.make_async_remote_copy(
+        src_ref=src,
+        dst_ref=dst,
+        send_sem=sems.at[0, slot],
+        recv_sem=sems.at[1, slot],
+        device_id=device,
+        device_id_type=pl.DeviceIdType.MESH,
+    )
+
+
+def greet(peers):
+    barrier = pltpu.get_barrier_semaphore()
+    for device in peers:
+        pl.semaphore_signal(barrier, inc=1, device_id=device, device_id_type=pl.DeviceIdType.MESH)
+    pl.semaphore_wait(barrier, len(peers))
+
+
+def halo_kernel(layers, count, across, mid, west, east, north, south, ncorn, scorn, sems):
+    tile_rows, tile_cols = mid.shape[1:]
+    row, col = lax.axis_index("row"), lax.axis_index("col")
+    below = (lax.rem(row + 1, count), col)
+    above = (lax.rem(row + count - 1, count), col)
+    toeast = (row, lax.rem(col + 1, across))
+    towest = (row, lax.rem(col + across - 1, across))
+    greet([below, above, toeast, towest])
+    last_rows = pl.ds(tile_rows - HALO, HALO)
+    first_rows = pl.ds(0, HALO)
+    last_cols = pl.ds(tile_cols - HALO, HALO)
+    first_cols = pl.ds(0, HALO)
+    sides, rows, corners = [], [], []
+    for l in range(layers):
+        ch = pl.ds(2 * l, 2)
+        slot = 8 * l
+        sides.append((
+            remote(mid.at[ch, :, last_cols], west.at[ch], sems, slot, toeast),
+            remote(mid.at[ch, :, first_cols], east.at[ch], sems, slot + 1, towest),
+        ))
+        rows.append(remote(mid.at[ch, last_rows], north.at[ch], sems, slot + 2, below))
+        rows.append(remote(mid.at[ch, first_rows], south.at[ch], sems, slot + 3, above))
+        for k, ref in enumerate((west, east)):
+            corners.append((
+                remote(ref.at[ch, last_rows], ncorn.at[k, ch], sems, slot + 4 + k, below),
+                remote(ref.at[ch, first_rows], scorn.at[k, ch], sems, slot + 6 + k, above),
+            ))
+    for pair in sides:
+        for copy in pair:
+            copy.start()
+    for copy in rows:
+        copy.start()
+    for l in range(layers):
+        for k in range(2):
+            sides[l][k].wait_recv()
+            for copy in corners[2 * l + k]:
+                copy.start()
+    for copy in rows:
+        copy.wait()
+    for pair in corners:
+        for copy in pair:
+            copy.wait()
+    for pair in sides:
+        for copy in pair:
+            copy.wait_send()
+
+
+def fetch_halo(layers, mid):
+    count, across = lax.axis_size("row"), lax.axis_size("col")
+    chans, tile_rows, tile_cols = mid.shape
+    side = (chans, tile_rows, HALO)
+    flat = (chans, HALO, tile_cols)
+    corner = (2, chans, HALO, HALO)
+    vmem = pl.BlockSpec(memory_space=pltpu.VMEM)
+    return pl.pallas_call(
+        functools.partial(halo_kernel, layers, count, across),
+        out_shape=[jax.ShapeDtypeStruct(s, F32) for s in (side, side, flat, flat, corner, corner)],
+        in_specs=[vmem],
+        out_specs=[vmem] * 6,
+        scratch_shapes=[pltpu.SemaphoreType.DMA((2, 8 * layers))],
+        compiler_params=pltpu.CompilerParams(
+            collective_id=0, has_side_effects=True, vmem_limit_bytes=24 * 2**20
+        ),
+        name="fetch_halo",
+    )(mid)
+
+
+def settle_kernel(
+    layers, count, across,
+    g_mid, g_west, g_east, g_north, g_south, g_ncorn, g_scorn, g_probe, out, probe,
+    south_corn, north_corn, side_send, side_recv, south_mid, north_mid,
+    probe_rows, probe_send, probe_cols, sems, row_sems, col_sems,
+):
+    tile_rows, tile_cols = out.shape[1:]
+    row, col = lax.axis_index("row"), lax.axis_index("col")
+    row_peers = [(lax.rem(row + d, count), col) for d in range(1, count)]
+    col_peers = [(row, lax.rem(col + d, across)) for d in range(1, across)]
+    below, above = row_peers[0], row_peers[-1]
+    toeast, towest = col_peers[0], col_peers[-1]
+    greet(row_peers + col_peers)
+    last_rows = pl.ds(tile_rows - HALO, HALO)
+    first_rows = pl.ds(0, HALO)
+    corners, mids = [], []
+    for l in reversed(range(layers)):
+        ch = pl.ds(2 * l, 2)
+        slot = 8 * l
+        for k in range(2):
+            corners.append((l, k, (
+                remote(g_ncorn.at[k, ch], south_corn.at[k, ch], sems, slot + k, above),
+                remote(g_scorn.at[k, ch], north_corn.at[k, ch], sems, slot + 2 + k, below),
+            )))
+        mids.append((l, (
+            remote(g_north.at[ch], south_mid.at[ch], sems, slot + 4, above),
+            remote(g_south.at[ch], north_mid.at[ch], sems, slot + 5, below),
+        )))
+    for _, _, pair in corners:
+        for copy in pair:
+            copy.start()
+    strip = probe.shape[1]
+    row_copies = []
+    for d in range(1, count):
+        device = row_peers[d - 1]
+        part = pl.ds(pl.multiple_of(device[0] * strip, strip), strip)
+        copy = remote(g_probe.at[:, part], probe_rows.at[d - 1], row_sems, d - 1, device)
+        copy.start()
+        row_copies.append(copy)
+    for _, pair in mids:
+        for copy in pair:
+            copy.start()
+    sides = []
+    for l, k, pair in corners:
+        ch = pl.ds(2 * l, 2)
+        for copy in pair:
+            copy.wait_recv()
+        side_send[k, ch] = (g_west, g_east)[k][ch]
+        side_send[k, ch, last_rows] += south_corn[k, ch]
+        side_send[k, ch, first_rows] += north_corn[k, ch]
+        copy = remote(
+            side_send.at[k, ch], side_recv.at[k, ch], sems, 8 * l + 6 + k, (towest, toeast)[k]
+        )
+        copy.start()
+        sides.append((l, k, copy))
+    total = g_probe[:, pl.ds(pl.multiple_of(row * strip, strip), strip)]
+    for d, copy in enumerate(row_copies):
+        copy.wait_recv()
+        total += probe_rows[d]
+    narrow = probe.shape[2]
+    for c in range(across):
+        probe_send[c] = total[:, :, c * narrow : (c + 1) * narrow]
+    col_copies = []
+    for d in range(1, across):
+        device = col_peers[d - 1]
+        copy = remote(probe_send.at[device[1]], probe_cols.at[d - 1], col_sems, d - 1, device)
+        copy.start()
+        col_copies.append(copy)
+    out[...] = g_mid[...]
+    for l, pair in mids:
+        ch = pl.ds(2 * l, 2)
+        for copy in pair:
+            copy.wait_recv()
+        out[ch, last_rows] += south_mid[ch]
+        out[ch, first_rows] += north_mid[ch]
+    for l, k, copy in sides:
+        ch = pl.ds(2 * l, 2)
+        cols = pl.ds((tile_cols - HALO) * (1 - k), HALO)
+        copy.wait_recv()
+        out[ch, :, cols] += side_recv[k, ch]
+    part = probe_send[col]
+    for d, copy in enumerate(col_copies):
+        copy.wait_recv()
+        part += probe_cols[d]
+    probe[...] = part
+    for _, _, pair in corners:
+        for copy in pair:
+            copy.wait_send()
+    for _, pair in mids:
+        for copy in pair:
+            copy.wait_send()
+    for _, _, copy in sides:
+        copy.wait_send()
+    for copy in row_copies + col_copies:
+        copy.wait_send()
+
+
+def settle(layers, grads):
+    count, across = lax.axis_size("row"), lax.axis_size("col")
+    chans, tile_rows, tile_cols = grads[0].shape
+    width = grads[7].shape[1]
+    strip, narrow = width // count, width // across
+    vmem = pl.BlockSpec(memory_space=pltpu.VMEM)
+    dma = pltpu.SemaphoreType.DMA
+    return pl.pallas_call(
+        functools.partial(settle_kernel, layers, count, across),
+        out_shape=[
+            jax.ShapeDtypeStruct((chans, tile_rows, tile_cols), F32),
+            jax.ShapeDtypeStruct((2, strip, narrow), F32),
+        ],
+        in_specs=[vmem] * 8,
+        out_specs=[vmem] * 2,
+        scratch_shapes=[
+            pltpu.VMEM((2, chans, HALO, HALO), F32),
+            pltpu.VMEM((2, chans, HALO, HALO), F32),
+            pltpu.VMEM((2, chans, tile_rows, HALO), F32),
+            pltpu.VMEM((2, chans, tile_rows, HALO), F32),
+            pltpu.VMEM((chans, HALO, tile_cols), F32),
+            pltpu.VMEM((chans, HALO, tile_cols), F32),
+            pltpu.VMEM((count - 1, 2, strip, width), F32),
+            pltpu.VMEM((across, 2, strip, narrow), F32),
+            pltpu.VMEM((across - 1, 2, strip, narrow), F32),
+            dma((2, 8 * layers)),
+            dma((2, count - 1)),
+            dma((2, across - 1)),
+        ],
+        compiler_params=pltpu.CompilerParams(
+            collective_id=1, has_side_effects=True, vmem_limit_bytes=40 * 2**20
+        ),
+        name="settle_gradients",
+    )(*grads)
 
 
 def body(specimen_transmit, illumination, fresnel_angle, recorded_intensity, frame_shifts):
@@ -177,46 +389,12 @@
     right, left = make_tables(width)
     filt = jnp.stack([jnp.cos(fresnel_angle), jnp.sin(fresnel_angle)])
     mid = specimen_transmit.reshape(2 * layers, tile, specimen_transmit.shape[3])
-    row_up, row_down = ring("row")
-    col_up, col_down = ring("col")
-    west = lax.ppermute(mid[:, :, -HALO:], "col", col_up)
-    east = lax.ppermute(mid[:, :, :HALO], "col", col_down)
-    north = lax.ppermute(mid[:, -HALO:], "row", row_up)
-    south = lax.ppermute(mid[:, :HALO], "row", row_down)
-    sides = jnp.stack([west, east])
-    ncorn = lax.ppermute(sides[:, :, -HALO:], "row", row_up)
-    scorn = lax.ppermute(sides[:, :, :HALO], "row", row_down)
-    pieces = (mid, west, east, north, south, ncorn, scorn)
-    g_mid, g_west, g_east, g_north, g_south, g_ncorn, g_scorn, g_probe = local_gradients(
+    pieces = (mid, *fetch_halo(layers, mid))
+    grads = local_gradients(
         layers, frame_shifts[0, 0], pieces, illumination, filt, recorded_intensity[0, 0], right, left
     )
-    from_south = lax.ppermute(g_ncorn, "row", row_down)
-    from_north = lax.ppermute(g_scorn, "row", row_up)
-    mid_south = lax.ppermute(g_north, "row", row_down)
-    mid_north = lax.ppermute(g_south, "row", row_up)
-    sides = jnp.stack([g_west, g_east])
-    sides = sides.at[:, :, -HALO:].add(from_south)
-    sides = sides.at[:, :, :HALO].add(from_north)
-    from_east = lax.ppermute(sides[0], "col", col_down)
-    from_west = lax.ppermute(sides[1], "col", col_up)
-    far = tile - HALO
-
-    def fit(x, low_row, low_col):
-        rows, cols = x.shape[1:]
-        pads = ((0, 0), (low_row, tile - rows - low_row), (low_col, tile - cols - low_col))
-        return jnp.pad(x, pads)
-
-    result = (
-        g_mid
-        + fit(mid_south, far, 0)
-        + fit(mid_north, 0, 0)
-        + fit(from_east, 0, far)
-        + fit(from_west, 0, 0)
-    )
-    result = result.reshape(specimen_transmit.shape)
-    partial_rows = lax.psum_scatter(g_probe, "row", scatter_dimension=1, tiled=True)
-    probe_part = lax.psum_scatter(partial_rows, "col", scatter_dimension=2, tiled=True)
-    return (result, probe_part)
+    result, probe_part = settle(layers, grads)
+    return (result.reshape(specimen_transmit.shape), probe_part)
 
 
 def solution(mesh):

time: 152 us -> 117 us (0.77)
  waiting for transfers between devices: 81.8 us -> 0 us
  Pallas kernels: 29.7 us -> 98 us
  starting transfers between devices: 13.7 us -> 0 us
  between operations: 14.2 us -> 0.69 us
  local copies, waits for them, and re-layouts: 7.31 us -> 16.9 us
  other arithmetic: 4.63 us -> 0.83 us
    pallas_call x0 -> x2, Pallas kernels: none -> 68.3 us  [the longest x1 36.8 us: settle(): pl.pallas_call(functools.partial(settle_kernel, layers, count, across), o...]
    ppermute x12 -> x0, waiting for transfers between devices: 45.3 us -> none  [the longest x1 11 us: body(): west = lax.ppermute(mid[:, :, -HALO:], 'col', col_up)]
    unnamed x3 -> x0, waiting for transfers between devices: 19.8 us -> none
    reduce_scatter x1 -> x0, waiting for transfers between devices: 16.7 us -> none  [body(): lax.psum_scatter(g_probe, 'row', scatter_dimension=1, tiled=True)]
    ppermute x12 -> x0, starting transfers between devices: 13.6 us -> none  [the longest x1 5.1 us: body(): east = lax.ppermute(mid[:, :, :HALO], 'col', col_down)]
    unnamed x26 -> x32, local copies, waits for them, and re-layouts: 4.87 us -> 14.9 us
    add x1 -> x0, other arithmetic: 2.34 us -> none  [body(): g_mid + fit(mid_south, far, 0) + fit(mid_north, 0, 0)]
  transfers between devices with their start and end apart: 14 -> 0, of which waited for: 8 -> 0; matrix products, arithmetic and copies ran while one was open for 4% -> 0% of each run, Pallas kernels for 0% -> 0%
where the time goes in v1:
time: 117 us; the launch traced here: 116 us
  Pallas kernels  98 us (84%)
  local copies, waits for them, and re-layouts  16.9 us (14%)
    pallas_call x1, Pallas kernels, settle(): pl.pallas_call(functools.partial(settle_kernel, layers, count, across), o...  36.8 us
    pallas_call x1, Pallas kernels, fetch_halo(): pl.pallas_call(functools.partial(halo_kernel, layers, count, across), out...  31.4 us
    pallas_call x1, Pallas kernels, local_gradients(): pl.pallas_call(functools.partial(local_kernel, layers), out_shape=[jax.Sh...  29.8 us
    unnamed x32, local copies, waits for them, and re-layouts  14.9 us

profile of v1, /device:TPU:0, one launch (start us, length us, event | category | flops | bytes accessed | tf_op | source)
XLA Modules:
  0.0 116.4 jit_solution(983171133800372891)
XLA Ops:
  0.6 0.0 copy-start
  0.6 1.9 %cosine_bitcast_fusion = (f32[1,256,256]{2,1,0:T(8,128)S(1)}, f32[1,256,256]{2,1,0:T(8,128)S(1)}) fusion(f32[256,256]{1,0:T(8,128)} %param.9), kind=kLoop, calls=%fused_computation.2 | loop fusion | bytes 786432 | tf_op jit(solution)/shard_map/stack | solution.py:390
  2.6 0.8 pad_maximum_fusion.filt
  3.4 0.0 copy-done
  3.4 31.4 %fetch_halo.1 = (f32[4,256,128]{2,1,0:T(8,128)S(1)}, f32[4,256,128]{2,1,0:T(8,128)S(1)}, f32[4,128,256]{2,1,0:T(8,128)S(1)}, f32[4,128,256]{2,1,0:T(8,128)S(1)},...) custom-call(f32[4,256,256]{2,1,0:T(8,128)S(1)} %bitcast.9), custom_call_target="tpu_custom_call" | custom-call | tf_op jit(solution)/shard_map/fetch_halo/pallas_call | solution.py:239
  34.9 0.0 copy-start.9
  34.9 0.8 copy-done.9
  35.7 0.0 copy-start.10
  35.7 0.8 copy-done.10
  36.5 0.0 copy-start.11
  36.5 0.8 copy-done.11
  37.3 0.0 copy-start.12
  37.3 0.8 copy-done.12
  38.1 0.0 copy-start.13
  38.1 0.8 copy-done.13
  38.9 0.0 copy-start.14
  38.9 0.8 copy-done.14
  39.7 29.8 %local_gradients.1 = (f32[4,256,256]{2,1,0:T(8,128)}, f32[4,256,128]{2,1,0:T(8,128)}, f32[4,256,128]{2,1,0:T(8,128)}, f32[4,128,256]{2,1,0:T(8,128)}, f32[4,128,...) custom-call(s32[2,2]{1,0:T(2,128)} %bitcast.12, ...), custom_call_target="tpu_custom_call" | custom-call | tf_op jit(solution)/shard_map/local_gradients/pallas_call | solution.py:152
  69.5 0.0 copy-start.1
  69.5 1.2 %copy-done.1 = f32[4,256,256]{2,1,0:T(8,128)S(1)} copy-done((f32[4,256,256]{2,1,0:T(8,128)S(1)}, f32[4,256,256]{2,1,0:T(8,128)}, u32[]{:S(2)}) %copy-start.1) | copy-done | bytes 1048600
  70.7 0.0 copy-start.2
  70.7 1.0 copy-done.2
  71.8 0.0 copy-start.3
  71.8 1.0 copy-done.3
  72.8 0.0 copy-start.4
  72.8 1.0 copy-done.4
  73.8 0.0 copy-start.5
  73.8 1.0 copy-done.5
  74.9 0.0 copy-start.6
  74.9 1.0 copy-done.6
  75.9 0.0 copy-start.7
  75.9 1.0 copy-done.7
  77.0 0.0 copy-start.8
  77.0 1.0 copy-done.8
  78.0 36.8 %settle_gradients.1 = (f32[4,256,256]{2,1,0:T(8,128)S(1)}, f32[2,32,64]{2,1,0:T(8,128)S(1)}) custom-call(f32[4,256,256]{2,1,0:T(8,128)S(1)} %copy-done.1, f32[4,256,128]{2,1,0:T(8,128)S(1)} %copy-done.2, f32[4,256,128]{2,1,0:T(8,128)S(1)} %copy-done.3, f32[4,128,256]{2,1,0:T(8,128)S(1)} %copy-done.4, f32[4,128,256]{2,1,0:T(8,128)S(1)} %copy-done.5, ...), custom_call_target="tpu_custom_call" | custom-call | tf_op jit(solution)/shard_map/settle_gradients/pallas_call | solution.py:356
  114.9 1.0 copy.11
  115.8 0.6 copy.12
Async XLA Ops:
  0.6 2.8 %copy-start = (f32[2,2,256,256]{3,2,1,0:T(8,128)S(1)}, f32[2,2,256,256]{3,2,1,0:T(8,128)}, u32[]{:S(2)}) copy-start(f32[2,2,256,256]{3,2,1,0:T(8,128)} %param.7) | copy-start | bytes 3145732
  34.9 0.8 copy-start.9
  35.7 0.8 copy-start.10
  36.5 0.8 copy-start.11
  37.3 0.8 copy-start.12
  38.1 0.8 copy-start.13
  38.9 0.8 copy-start.14
  69.5 1.2 %copy-start.1 = (f32[4,256,256]{2,1,0:T(8,128)S(1)}, f32[4,256,256]{2,1,0:T(8,128)}, u32[]{:S(2)}) copy-start(f32[4,256,256]{2,1,0:T(8,128)} %get-tuple-element.24.g_mid) | copy-start | bytes 3145732
  70.7 1.0 copy-start.2
  71.8 1.0 copy-start.3
  72.8 1.0 copy-start.4
  73.8 1.0 copy-start.5
  74.9 1.0 copy-start.6
  75.9 1.0 copy-start.7
  77.0 1.0 copy-start.8

commit v2 on v1

--- a/solution.py
+++ b/solution.py
@@ -159,7 +159,7 @@
             pltpu.VMEM((chans, side + ROWS, side), F32),
             pltpu.VMEM((chans, width, width), F32),
         ],
-        compiler_params=pltpu.CompilerParams(vmem_limit_bytes=56 * 2**20),
+        compiler_params=pltpu.CompilerParams(vmem_limit_bytes=34 * 2**20),
         name="local_gradients",
     )(shifts, *pieces, illum, filt, seen, right, left)
 
@@ -182,7 +182,9 @@
     pl.semaphore_wait(barrier, len(peers))
 
 
-def halo_kernel(layers, count, across, mid, west, east, north, south, ncorn, scorn, sems):
+def halo_kernel(
+    layers, count, across, mid, angle, west, east, north, south, ncorn, scorn, filt, sems
+):
     tile_rows, tile_cols = mid.shape[1:]
     row, col = lax.axis_index("row"), lax.axis_index("col")
     below = (lax.rem(row + 1, count), col)
@@ -214,6 +216,8 @@
             copy.start()
     for copy in rows:
         copy.start()
+    filt[0] = jnp.cos(angle[...])
+    filt[1] = jnp.sin(angle[...])
     for l in range(layers):
         for k in range(2):
             sides[l][k].wait_recv()
@@ -229,7 +233,7 @@
             copy.wait_send()
 
 
-def fetch_halo(layers, mid):
+def fetch_halo(layers, mid, angle):
     count, across = lax.axis_size("row"), lax.axis_size("col")
     chans, tile_rows, tile_cols = mid.shape
     side = (chans, tile_rows, HALO)
@@ -238,15 +242,18 @@
     vmem = pl.BlockSpec(memory_space=pltpu.VMEM)
     return pl.pallas_call(
         functools.partial(halo_kernel, layers, count, across),
-        out_shape=[jax.ShapeDtypeStruct(s, F32) for s in (side, side, flat, flat, corner, corner)],
-        in_specs=[vmem],
-        out_specs=[vmem] * 6,
+        out_shape=[
+            jax.ShapeDtypeStruct(s, F32)
+            for s in (side, side, flat, flat, corner, corner, (2, *angle.shape))
+        ],
+        in_specs=[vmem] * 2,
+        out_specs=[vmem] * 7,
         scratch_shapes=[pltpu.SemaphoreType.DMA((2, 8 * layers))],
         compiler_params=pltpu.CompilerParams(
             collective_id=0, has_side_effects=True, vmem_limit_bytes=24 * 2**20
         ),
         name="fetch_halo",
-    )(mid)
+    )(mid, angle)
 
 
 def settle_kernel(
@@ -376,7 +383,7 @@
             dma((2, across - 1)),
         ],
         compiler_params=pltpu.CompilerParams(
-            collective_id=1, has_side_effects=True, vmem_limit_bytes=40 * 2**20
+            collective_id=1, has_side_effects=True, vmem_limit_bytes=30 * 2**20
         ),
         name="settle_gradients",
     )(*grads)
@@ -387,9 +394,9 @@
     tile = specimen_transmit.shape[2]
     width = illumination.shape[1]
     right, left = make_tables(width)
-    filt = jnp.stack([jnp.cos(fresnel_angle), jnp.sin(fresnel_angle)])
     mid = specimen_transmit.reshape(2 * layers, tile, specimen_transmit.shape[3])
-    pieces = (mid, *fetch_halo(layers, mid))
+    *halo, filt = fetch_halo(layers, mid, fresnel_angle)
+    pieces = (mid, *halo)
     grads = local_gradients(
         layers, frame_shifts[0, 0], pieces, illumination, filt, recorded_intensity[0, 0], right, left
     )

time: 117 us -> 104 us (0.89)
  local copies, waits for them, and re-layouts: 16.9 us -> 8.77 us
  Pallas kernels: 98 us -> 94 us
    unnamed x32 -> x18, local copies, waits for them, and re-layouts: 14.9 us -> 8.77 us
    pallas_call x1, Pallas kernels: 29.8 us -> 25.6 us  [local_gradients(): pl.pallas_call(functools.partial(local_kernel, layers), out_shape=[jax.Sh...]
    another operation x1 -> x0, local copies, waits for them, and re-layouts: 1.94 us -> none  [body(): filt = jnp.stack([jnp.cos(fresnel_angle), jnp.sin(fresnel_angle)])]
where the time goes in v2:
time: 104 us; the launch traced here: 103 us
  Pallas kernels  94 us (90%)
  local copies, waits for them, and re-layouts  8.77 us (8%)
    pallas_call x1, Pallas kernels, settle(): pl.pallas_call(functools.partial(settle_kernel, layers, count, across), o...  37 us
    pallas_call x1, Pallas kernels, fetch_halo(): pl.pallas_call(functools.partial(halo_kernel, layers, count, across), out...  31.4 us
    pallas_call x1, Pallas kernels, local_gradients(): pl.pallas_call(functools.partial(local_kernel, layers), out_shape=[jax.Sh...  25.6 us
    unnamed x18, local copies, waits for them, and re-layouts  8.77 us

profile of v2, /device:TPU:0, one launch (start us, length us, event | category | flops | bytes accessed | tf_op | source)
XLA Modules:
  0.0 103.5 jit_solution(3154310357004395703)
XLA Ops:
  0.6 0.0 copy-start
  0.6 1.2 %copy-done = f32[2,2,256,256]{3,2,1,0:T(8,128)S(1)} copy-done((f32[2,2,256,256]{3,2,1,0:T(8,128)S(1)}, f32[2,2,256,256]{3,2,1,0:T(8,128)}, u32[]{:S(2)}) %copy-start) | copy-done | bytes 1048600
  1.9 0.0 copy-start.6
  1.9 0.9 copy-done.6
  2.8 0.0 copy-start.1
  2.8 31.4 %fetch_halo.1 = (f32[4,256,128]{2,1,0:T(8,128)S(1)}, f32[4,256,128]{2,1,0:T(8,128)S(1)}, f32[4,128,256]{2,1,0:T(8,128)S(1)}, f32[4,128,256]{2,1,0:T(8,128)S(1)},...) custom-call(f32[4,256,256]{2,1,0:T(8,128)S(1)} %bitcast.4, ...), custom_call_target="tpu_custom_call" | custom-call | tf_op jit(solution)/shard_map/fetch_halo/pallas_call | solution.py:243
  34.2 0.0 copy-start.7
  34.3 0.0 copy-done.1
  34.3 0.7 copy-done.7
  34.9 0.0 copy-start.2
  34.9 1.1 %copy-done.2 = bf16[256,1536]{1,0:T(8,128)(2,1)S(1)} copy-done((bf16[256,1536]{1,0:T(8,128)(2,1)S(1)}, bf16[256,1536]{1,0:T(8,128)(2,1)}, u32[]{:S(2)}) %copy-start.2) | copy-done | bytes 786456
  36.1 0.0 copy-start.3
  36.1 1.1 %copy-done.3 = bf16[1536,256]{1,0:T(8,128)(2,1)S(1)} copy-done((bf16[1536,256]{1,0:T(8,128)(2,1)S(1)}, bf16[1536,256]{1,0:T(8,128)(2,1)}, u32[]{:S(2)}) %copy-start.3) | copy-done | bytes 786456
  37.2 0.0 copy-start.4
  37.2 1.0 %copy-done.4 = f32[2,256,256]{2,1,0:T(8,128)S(1)} copy-done((f32[2,256,256]{2,1,0:T(8,128)S(1)}, f32[2,256,256]{2,1,0:T(8,128)}, u32[]{:S(2)}) %copy-start.4) | copy-done | bytes 524312
  38.2 0.0 copy-start.5
  38.2 1.0 %copy-done.5 = f32[1,1,2,256,256]{4,3,2,1,0:T(8,128)S(1)} copy-done((f32[1,1,2,256,256]{4,3,2,1,0:T(8,128)S(1)}, f32[1,1,2,256,256]{4,3,2,1,0:T(8,128)}, u32[]{:S(2)}) %copy-start.5) | copy-done | bytes 524312
  39.3 25.6 %local_gradients.1 = (f32[4,256,256]{2,1,0:T(8,128)S(1)}, f32[4,256,128]{2,1,0:T(8,128)S(1)}, f32[4,256,128]{2,1,0:T(8,128)S(1)}, f32[4,128,256]{2,1,0:T(8,128)S...) custom-call(s32[2,2]{1,0:T(2,128)S(1)} %bitcast.8, ...), custom_call_target="tpu_custom_call" | custom-call | tf_op jit(solution)/shard_map/local_gradients/pallas_call | solution.py:152
  64.9 37.0 %settle_gradients.1 = (f32[4,256,256]{2,1,0:T(8,128)S(1)}, f32[2,32,64]{2,1,0:T(8,128)S(1)}) custom-call(f32[4,256,256]{2,1,0:T(8,128)S(1)} %get-tuple-element.26.g_mid, f32[4,256,128]{2,1,0:T(8,128)S(1)} %get-tuple-element.27.g_west, f32[4,256,128]{2,1,0:T(8,128)S(1)} %get-tuple-element.28.g_east, f32[4,128,256]{2,1,0:T(8,128)S(1)} %get-tuple-element.29.g_north, ...), custom_call_target="tpu_custom_call" | custom-call | tf_op jit(solution)/shard_map/settle_gradients/pallas_call | solution.py:363
  101.9 1.0 copy.11
  102.8 0.6 copy.12
Async XLA Ops:
  0.6 1.2 %copy-start = (f32[2,2,256,256]{3,2,1,0:T(8,128)S(1)}, f32[2,2,256,256]{3,2,1,0:T(8,128)}, u32[]{:S(2)}) copy-start(f32[2,2,256,256]{3,2,1,0:T(8,128)} %param.7) | copy-start | bytes 3145732
  1.9 0.9 copy-start.6
  2.8 31.5 %copy-start.1 = (f32[2,2,256,256]{3,2,1,0:T(8,128)S(1)}, f32[2,2,256,256]{3,2,1,0:T(8,128)}, u32[]{:S(2)}) copy-start(f32[2,2,256,256]{3,2,1,0:T(8,128)} %param.7) | copy-start | bytes 3145732
  34.2 0.7 copy-start.7
  34.9 1.1 %copy-start.2 = (bf16[256,1536]{1,0:T(8,128)(2,1)S(1)}, bf16[256,1536]{1,0:T(8,128)(2,1)}, u32[]{:S(2)}) copy-start(bf16[256,1536]{1,0:T(8,128)(2,1)} %constant.5.clone.left) | copy-start | bytes 2359300
  36.1 1.1 %copy-start.3 = (bf16[1536,256]{1,0:T(8,128)(2,1)S(1)}, bf16[1536,256]{1,0:T(8,128)(2,1)}, u32[]{:S(2)}) copy-start(bf16[1536,256]{1,0:T(8,128)(2,1)} %constant.4.clone.right) | copy-start | bytes 2359300
  37.2 1.0 %copy-start.4 = (f32[2,256,256]{2,1,0:T(8,128)S(1)}, f32[2,256,256]{2,1,0:T(8,128)}, u32[]{:S(2)}) copy-start(f32[2,256,256]{2,1,0:T(8,128)} %illum.1) | copy-start | bytes 1572868
  38.2 1.0 %copy-start.5 = (f32[1,1,2,256,256]{4,3,2,1,0:T(8,128)S(1)}, f32[1,1,2,256,256]{4,3,2,1,0:T(8,128)}, u32[]{:S(2)}) copy-start(f32[1,1,2,256,256]{4,3,2,1,0:T(8,128)} %param.10) | copy-start | bytes 1572868

commit v3 on v2

--- a/solution.py
+++ b/solution.py
@@ -183,7 +183,7 @@
 
 
 def halo_kernel(
-    layers, count, across, mid, angle, west, east, north, south, ncorn, scorn, filt, sems
+    chans, count, across, mid, angle, west, east, north, south, ncorn, scorn, filt, sems
 ):
     tile_rows, tile_cols = mid.shape[1:]
     row, col = lax.axis_index("row"), lax.axis_index("col")
@@ -197,8 +197,8 @@
     last_cols = pl.ds(tile_cols - HALO, HALO)
     first_cols = pl.ds(0, HALO)
     sides, rows, corners = [], [], []
-    for l in range(layers):
-        ch = pl.ds(2 * l, 2)
+    for l in range(chans):
+        ch = pl.ds(l, 1)
         slot = 8 * l
         sides.append((
             remote(mid.at[ch, :, last_cols], west.at[ch], sems, slot, toeast),
@@ -218,7 +218,7 @@
         copy.start()
     filt[0] = jnp.cos(angle[...])
     filt[1] = jnp.sin(angle[...])
-    for l in range(layers):
+    for l in range(chans):
         for k in range(2):
             sides[l][k].wait_recv()
             for copy in corners[2 * l + k]:
@@ -233,7 +233,7 @@
             copy.wait_send()
 
 
-def fetch_halo(layers, mid, angle):
+def fetch_halo(mid, angle):
     count, across = lax.axis_size("row"), lax.axis_size("col")
     chans, tile_rows, tile_cols = mid.shape
     side = (chans, tile_rows, HALO)
@@ -241,14 +241,14 @@
     corner = (2, chans, HALO, HALO)
     vmem = pl.BlockSpec(memory_space=pltpu.VMEM)
     return pl.pallas_call(
-        functools.partial(halo_kernel, layers, count, across),
+        functools.partial(halo_kernel, chans, count, across),
         out_shape=[
             jax.ShapeDtypeStruct(s, F32)
             for s in (side, side, flat, flat, corner, corner, (2, *angle.shape))
         ],
         in_specs=[vmem] * 2,
         out_specs=[vmem] * 7,
-        scratch_shapes=[pltpu.SemaphoreType.DMA((2, 8 * layers))],
+        scratch_shapes=[pltpu.SemaphoreType.DMA((2, 8 * chans))],
         compiler_params=pltpu.CompilerParams(
             collective_id=0, has_side_effects=True, vmem_limit_bytes=24 * 2**20
         ),
@@ -257,7 +257,7 @@
 
 
 def settle_kernel(
-    layers, count, across,
+    chans, count, across,
     g_mid, g_west, g_east, g_north, g_south, g_ncorn, g_scorn, g_probe, out, probe,
     south_corn, north_corn, side_send, side_recv, south_mid, north_mid,
     probe_rows, probe_send, probe_cols, sems, row_sems, col_sems,
@@ -272,8 +272,8 @@
     last_rows = pl.ds(tile_rows - HALO, HALO)
     first_rows = pl.ds(0, HALO)
     corners, mids = [], []
-    for l in reversed(range(layers)):
-        ch = pl.ds(2 * l, 2)
+    for l in range(chans):
+        ch = pl.ds(l, 1)
         slot = 8 * l
         for k in range(2):
             corners.append((l, k, (
@@ -287,6 +287,19 @@
     for _, _, pair in corners:
         for copy in pair:
             copy.start()
+    sides = []
+    for l, k, pair in corners:
+        ch = pl.ds(l, 1)
+        for copy in pair:
+            copy.wait_recv()
+        side_send[k, ch] = (g_west, g_east)[k][ch]
+        side_send[k, ch, last_rows] += south_corn[k, ch]
+        side_send[k, ch, first_rows] += north_corn[k, ch]
+        copy = remote(
+            side_send.at[k, ch], side_recv.at[k, ch], sems, 8 * l + 6 + k, (towest, toeast)[k]
+        )
+        copy.start()
+        sides.append((l, k, copy))
     strip = probe.shape[1]
     row_copies = []
     for d in range(1, count):
@@ -298,19 +311,6 @@
     for _, pair in mids:
         for copy in pair:
             copy.start()
-    sides = []
-    for l, k, pair in corners:
-        ch = pl.ds(2 * l, 2)
-        for copy in pair:
-            copy.wait_recv()
-        side_send[k, ch] = (g_west, g_east)[k][ch]
-        side_send[k, ch, last_rows] += south_corn[k, ch]
-        side_send[k, ch, first_rows] += north_corn[k, ch]
-        copy = remote(
-            side_send.at[k, ch], side_recv.at[k, ch], sems, 8 * l + 6 + k, (towest, toeast)[k]
-        )
-        copy.start()
-        sides.append((l, k, copy))
     total = g_probe[:, pl.ds(pl.multiple_of(row * strip, strip), strip)]
     for d, copy in enumerate(row_copies):
         copy.wait_recv()
@@ -326,13 +326,13 @@
         col_copies.append(copy)
     out[...] = g_mid[...]
     for l, pair in mids:
-        ch = pl.ds(2 * l, 2)
+        ch = pl.ds(l, 1)
         for copy in pair:
             copy.wait_recv()
         out[ch, last_rows] += south_mid[ch]
         out[ch, first_rows] += north_mid[ch]
     for l, k, copy in sides:
-        ch = pl.ds(2 * l, 2)
+        ch = pl.ds(l, 1)
         cols = pl.ds((tile_cols - HALO) * (1 - k), HALO)
         copy.wait_recv()
         out[ch, :, cols] += side_recv[k, ch]
@@ -353,7 +353,7 @@
         copy.wait_send()
 
 
-def settle(layers, grads):
+def settle(grads):
     count, across = lax.axis_size("row"), lax.axis_size("col")
     chans, tile_rows, tile_cols = grads[0].shape
     width = grads[7].shape[1]
@@ -361,7 +361,7 @@
     vmem = pl.BlockSpec(memory_space=pltpu.VMEM)
     dma = pltpu.SemaphoreType.DMA
     return pl.pallas_call(
-        functools.partial(settle_kernel, layers, count, across),
+        functools.partial(settle_kernel, chans, count, across),
         out_shape=[
             jax.ShapeDtypeStruct((chans, tile_rows, tile_cols), F32),
             jax.ShapeDtypeStruct((2, strip, narrow), F32),
@@ -378,7 +378,7 @@
             pltpu.VMEM((count - 1, 2, strip, width), F32),
             pltpu.VMEM((across, 2, strip, narrow), F32),
             pltpu.VMEM((across - 1, 2, strip, narrow), F32),
-            dma((2, 8 * layers)),
+            dma((2, 8 * chans)),
             dma((2, count - 1)),
             dma((2, across - 1)),
         ],
@@ -395,12 +395,12 @@
     width = illumination.shape[1]
     right, left = make_tables(width)
     mid = specimen_transmit.reshape(2 * layers, tile, specimen_transmit.shape[3])
-    *halo, filt = fetch_halo(layers, mid, fresnel_angle)
+    *halo, filt = fetch_halo(mid, fresnel_angle)
     pieces = (mid, *halo)
     grads = local_gradients(
         layers, frame_shifts[0, 0], pieces, illumination, filt, recorded_intensity[0, 0], right, left
     )
-    result, probe_part = settle(layers, grads)
+    result, probe_part = settle(grads)
     return (result.reshape(specimen_transmit.shape), probe_part)
 
 

time: 104 us -> 104 us (level)
  no operation moved by 1% of the time
where the time goes in v3:
time: 104 us
  Pallas kernels  94.5 us (91%)
  local copies, waits for them, and re-layouts  8.77 us (8%)
    pallas_call x1, Pallas kernels, settle(): pl.pallas_call(functools.partial(settle_kernel, chans, count, across), ou...  37.6 us
    pallas_call x1, Pallas kernels, fetch_halo(): pl.pallas_call(functools.partial(halo_kernel, chans, count, across), out_...  31.3 us
    pallas_call x1, Pallas kernels, local_gradients(): pl.pallas_call(functools.partial(local_kernel, layers), out_shape=[jax.Sh...  25.6 us
    unnamed x18, local copies, waits for them, and re-layouts  8.77 us

profile of v3, /device:TPU:0, one launch (start us, length us, event | category | flops | bytes accessed | tf_op | source)
XLA Modules:
  0.0 103.9 jit_solution(11451028342056871649)
XLA Ops:
  0.6 0.0 copy-start
  0.6 1.2 %copy-done = f32[2,2,256,256]{3,2,1,0:T(8,128)S(1)} copy-done((f32[2,2,256,256]{3,2,1,0:T(8,128)S(1)}, f32[2,2,256,256]{3,2,1,0:T(8,128)}, u32[]{:S(2)}) %copy-start) | copy-done | bytes 1048600
  1.9 0.0 copy-start.6
  1.9 0.9 copy-done.6
  2.8 0.0 copy-start.1
  2.8 31.3 %fetch_halo.1 = (f32[4,256,128]{2,1,0:T(8,128)S(1)}, f32[4,256,128]{2,1,0:T(8,128)S(1)}, f32[4,128,256]{2,1,0:T(8,128)S(1)}, f32[4,128,256]{2,1,0:T(8,128)S(1)},...) custom-call(f32[4,256,256]{2,1,0:T(8,128)S(1)} %bitcast.4, ...), custom_call_target="tpu_custom_call" | custom-call | tf_op jit(solution)/shard_map/fetch_halo/pallas_call | solution.py:243
  34.1 0.0 copy-start.7
  34.1 0.0 copy-done.1
  34.1 0.7 copy-done.7
  34.8 0.0 copy-start.2
  34.8 1.1 %copy-done.2 = bf16[256,1536]{1,0:T(8,128)(2,1)S(1)} copy-done((bf16[256,1536]{1,0:T(8,128)(2,1)S(1)}, bf16[256,1536]{1,0:T(8,128)(2,1)}, u32[]{:S(2)}) %copy-start.2) | copy-done | bytes 786456
  35.9 0.0 copy-start.3
  35.9 1.1 %copy-done.3 = bf16[1536,256]{1,0:T(8,128)(2,1)S(1)} copy-done((bf16[1536,256]{1,0:T(8,128)(2,1)S(1)}, bf16[1536,256]{1,0:T(8,128)(2,1)}, u32[]{:S(2)}) %copy-start.3) | copy-done | bytes 786456
  37.0 0.0 copy-start.4
  37.0 1.0 %copy-done.4 = f32[2,256,256]{2,1,0:T(8,128)S(1)} copy-done((f32[2,256,256]{2,1,0:T(8,128)S(1)}, f32[2,256,256]{2,1,0:T(8,128)}, u32[]{:S(2)}) %copy-start.4) | copy-done | bytes 524312
  38.1 0.0 copy-start.5
  38.1 1.0 %copy-done.5 = f32[1,1,2,256,256]{4,3,2,1,0:T(8,128)S(1)} copy-done((f32[1,1,2,256,256]{4,3,2,1,0:T(8,128)S(1)}, f32[1,1,2,256,256]{4,3,2,1,0:T(8,128)}, u32[]{:S(2)}) %copy-start.5) | copy-done | bytes 524312
  39.1 25.6 %local_gradients.1 = (f32[4,256,256]{2,1,0:T(8,128)S(1)}, f32[4,256,128]{2,1,0:T(8,128)S(1)}, f32[4,256,128]{2,1,0:T(8,128)S(1)}, f32[4,128,256]{2,1,0:T(8,128)S...) custom-call(s32[2,2]{1,0:T(2,128)S(1)} %bitcast.8, ...), custom_call_target="tpu_custom_call" | custom-call | tf_op jit(solution)/shard_map/local_gradients/pallas_call | solution.py:152
  64.7 37.6 %settle_gradients.1 = (f32[4,256,256]{2,1,0:T(8,128)S(1)}, f32[2,32,64]{2,1,0:T(8,128)S(1)}) custom-call(f32[4,256,256]{2,1,0:T(8,128)S(1)} %get-tuple-element.26.g_mid, f32[4,256,128]{2,1,0:T(8,128)S(1)} %get-tuple-element.27.g_west, f32[4,256,128]{2,1,0:T(8,128)S(1)} %get-tuple-element.28.g_east, f32[4,128,256]{2,1,0:T(8,128)S(1)} %get-tuple-element.29.g_north, ...), custom_call_target="tpu_custom_call" | custom-call | tf_op jit(solution)/shard_map/settle_gradients/pallas_call | solution.py:363
  102.3 1.0 copy.11
  103.3 0.6 copy.12
Async XLA Ops:
  0.6 1.2 %copy-start = (f32[2,2,256,256]{3,2,1,0:T(8,128)S(1)}, f32[2,2,256,256]{3,2,1,0:T(8,128)}, u32[]{:S(2)}) copy-start(f32[2,2,256,256]{3,2,1,0:T(8,128)} %param.7) | copy-start | bytes 3145732
  1.9 0.9 copy-start.6
  2.8 31.3 %copy-start.1 = (f32[2,2,256,256]{3,2,1,0:T(8,128)S(1)}, f32[2,2,256,256]{3,2,1,0:T(8,128)}, u32[]{:S(2)}) copy-start(f32[2,2,256,256]{3,2,1,0:T(8,128)} %param.7) | copy-start | bytes 3145732
  34.1 0.7 copy-start.7
  34.8 1.1 %copy-start.2 = (bf16[256,1536]{1,0:T(8,128)(2,1)S(1)}, bf16[256,1536]{1,0:T(8,128)(2,1)}, u32[]{:S(2)}) copy-start(bf16[256,1536]{1,0:T(8,128)(2,1)} %constant.5.clone.left) | copy-start | bytes 2359300
  35.9 1.1 %copy-start.3 = (bf16[1536,256]{1,0:T(8,128)(2,1)S(1)}, bf16[1536,256]{1,0:T(8,128)(2,1)}, u32[]{:S(2)}) copy-start(bf16[1536,256]{1,0:T(8,128)(2,1)} %constant.4.clone.right) | copy-start | bytes 2359300
  37.0 1.0 %copy-start.4 = (f32[2,256,256]{2,1,0:T(8,128)S(1)}, f32[2,256,256]{2,1,0:T(8,128)}, u32[]{:S(2)}) copy-start(f32[2,256,256]{2,1,0:T(8,128)} %illum.1) | copy-start | bytes 1572868
  38.1 1.0 %copy-start.5 = (f32[1,1,2,256,256]{4,3,2,1,0:T(8,128)S(1)}, f32[1,1,2,256,256]{4,3,2,1,0:T(8,128)}, u32[]{:S(2)}) copy-start(f32[1,1,2,256,256]{4,3,2,1,0:T(8,128)} %param.10) | copy-start | bytes 1572868
